TPU v7x, 32 devices: a whole 2x2x4 slice. The times are simulated.
32 devices in a mesh: dp: 8 (over z, core), pos: 4 (over y, x).
Axes of the slice: x: 2, y: 2, z: 4, core: 2. Of those that a mesh axis runs over, the one named last changes fastest.
Arguments:
- features: bfloat16 [64, 128, 224], P(('dp', 'pos')), may hold values from -6 to 6
- counts: int32 [32], P(('dp', 'pos')), may hold values from 1 to 2, as said below
- channel_order: int32 [224], replicated, may hold values from 0 to 223, each once
Outputs:
- mean: float32 [128, 100], P('pos')
- covariance: float32 [128, 100, 100], P('pos')
Inputs may be any that keep to these rules, and one draw needn't show every extreme that they name: `counts`: some device has all 2 slots live and some device only one.
All inputs are finite; a program needn't handle non-finite values.
Results may differ from a plain program's by a relative error of at most 0.0003.
Values may be sent and summed in bfloat16 or wider, within the bound.
No kernel may reach another device: no remote copies, remote signals or barrier semaphores. Data moves between devices by JAX's collectives and lax.ppermute only.
A program may use at most 128 MiB of HBM per device.

v0:
```python
import jax
import jax.numpy as jnp
from jax import lax
from jax.sharding import PartitionSpec as P

CH = 100


def local_stats(received, source_counts, slots, rows, width):
    sources = source_counts.shape[0]
    samples = received.reshape(sources * slots, rows, width).astype(jnp.float32)
    live_mask = (jnp.arange(slots, dtype=jnp.float32)[None, :] < source_counts[:, None]).astype(
        jnp.float32
    )
    live_mask = live_mask.reshape(sources * slots)
    group_count = jnp.sum(source_counts).reshape(1)
    group_sums = jnp.sum(samples, axis=0)
    group_mean = group_sums / group_count
    centered = (samples - group_mean[None]) * live_mask[:, None, None]
    products = jnp.einsum("gpc,gpd->pcd", centered, centered, precision=lax.Precision.HIGHEST)
    return (group_count, group_sums, group_mean, products)


def common_mean(group_count, group_sums, group_mean):
    total_count, total_sums = lax.psum((group_count, group_sums), "dp")
    mean = total_sums / total_count
    offset = group_mean - mean
    weighted = offset * group_count
    return (total_count, mean, offset, weighted)


def on_device(features, counts, channel_order):
    slots, positions, channels = features.shape
    groups = lax.axis_size("pos")
    pos_dev = positions // groups
    kept = channel_order[:CH]
    picker = (kept[None, :] == jnp.arange(channels, dtype=jnp.int32)[:, None]).astype(jnp.bfloat16)
    owned = counts[0]
    slot_live = (jnp.arange(slots, dtype=jnp.int32) < owned).astype(jnp.bfloat16)
    embed = jnp.dot(
        features.reshape(slots * positions, channels), picker, preferred_element_type=jnp.float32
    )
    embed = embed.astype(jnp.bfloat16).reshape(slots, positions, CH) * slot_live[:, None, None]
    identity = jnp.eye(CH, dtype=jnp.float32)
    packed = embed.reshape(slots, groups, pos_dev * CH)
    owned_wire = jnp.broadcast_to(owned.astype(jnp.bfloat16).reshape(1, 1, 1), (1, groups, 1))
    received, source_counts = (
        lax.all_to_all(packed, "pos", split_axis=1, concat_axis=0, tiled=True),
        lax.all_to_all(owned_wire, "pos", split_axis=1, concat_axis=0, tiled=True),
    )
    source_counts = source_counts.reshape(groups).astype(jnp.float32)
    group_count, group_sums, group_mean, products = local_stats(
        received, source_counts, slots, pos_dev, CH
    )
    total_count, mean, offset, weighted = common_mean(group_count, group_sums, group_mean)
    own_term = products + offset[:, :, None] * weighted[:, None, :]
    summed = lax.psum(own_term, "dp")
    covariance = summed / (total_count[0] - 1.0) + 0.01 * identity
    return (mean, covariance)


def solution(mesh):
    in_specs = (P(("dp", "pos"), None, None), P(("dp", "pos")), P())
    out_specs = (P("pos", None), P("pos", None, None))
    return jax.shard_map(
        on_device, mesh=mesh, in_specs=in_specs, out_specs=out_specs, check_vma=False
    )
```

profile of v0, /device:TPU:0, one launch (start us, length us, event | category | flops | bytes accessed | tf_op | source)
XLA Modules:
  0.0 129.7 jit_solution(13337276662901932767)
XLA Ops:
  7.2 0.0 copy-start
  7.9 0.6 broadcast_in_dim.2
  8.4 5.2 %all-to-all-start.1 = ((bf16[1,4,1]{2,0,1:T(2,128)(2,1)}), bf16[1,4,1]{2,0,1:T(2,128)(2,1)S(1)}, u32[]{:S(2)}, u32[]{:S(2)}) async-start(bf16[1,4,1]{2,0,1:T(2,128)(2,1)} %broadcast_in_dim.2), calls=%async_computation.1 | async-start | bytes 4096 | tf_op jit(solution)/shard_map/all_to_all | solution.py:49
  13.6 0.7 slice.3
  14.3 0.0 copy-done
  14.3 0.2 fusion
  14.5 0.1 copy.19
  14.6 0.2 reshape.81
  14.8 0.1 broadcast_multiply_fusion
  14.9 0.7 copy.20
  15.6 2.6 %all-to-all-done.1 = bf16[1,4,1]{2,0,1:T(2,128)(2,1)S(1)} async-done(((bf16[1,4,1]{2,0,1:T(2,128)(2,1)}), bf16[1,4,1]{2,0,1:T(2,128)(2,1)S(1)}, u32[]{:S(2)}, u32[]{:S(2)}) %all-to-all-start.1) | async-done | bytes 40 | tf_op jit(solution)/shard_map/all_to_all | solution.py:49
  18.2 3.3 %all-to-all-start = ((bf16[2,4,3200]{2,0,1:T(2,128)(2,1)}), bf16[2,4,3200]{2,0,1:T(2,128)(2,1)S(1)}, u32[]{:S(2)}, u32[]{:S(2)}) async-start(bf16[2,4,3200]{2,0,1:T(2,128)(2,1)} %copy.20), calls=%async_computation | async-start | bytes 102400 | tf_op jit(solution)/shard_map/all_to_all | solution.py:48
  21.5 0.0 all-reduce.3.cloned.1.call-start
  21.5 0.7 convert_reduce_fusion.1
  22.2 0.1 fusion.6
  22.3 0.1 reshape.85
  22.4 3.9 %all-to-all-done = bf16[2,4,3200]{2,0,1:T(2,128)(2,1)S(1)} async-done(((bf16[2,4,3200]{2,0,1:T(2,128)(2,1)}), bf16[2,4,3200]{2,0,1:T(2,128)(2,1)S(1)}, u32[]{:S(2)}, u32[]{:S(2)}) %all-to-all-start) | async-done | bytes 51232 | tf_op jit(solution)/shard_map/all_to_all | solution.py:48
  26.2 0.1 convert_reduce_fusion
  26.3 0.1 reduce_sum.21
  26.5 0.3 reshape.84
  26.7 27.4 %all-reduce = (f32[32,100]{1,0:T(8,128)S(1)}, f32[]{:T(128)}) all-reduce(f32[32,100]{1,0:T(8,128)S(1)} %reduce_sum.21, f32[]{:T(128)} %get-tuple-element.11), channel_id=1, replica_groups=mesh['dp'=8,'pos'=4] {'dp'}, use_global_device_ids=true, to_apply=%region_1.0 | all-reduce | flops 3201 | bytes 25608 | tf_op jit(solution)/shard_map/psum | solution.py:25
  54.2 1.9 %broadcast_multiply_fusion.1 = (f32[32,100]{1,0:T(8,128)S(1)}, f32[32,100]{1,0:T(8,128)S(1)}, f32[32,100]{1,0:T(8,128)S(1)}, f32[32,100]{1,0:T(8,128)}) fusion(f32[]{:T(128)} %get-tuple-element.11, f32[32,100]{1,0:T(8,128)S(1)} %reduce_sum.21, f32[32,100]{1,0:T(8,128)S(1)} %get-tuple-element.12, f32[]{:T(128)} %get-tuple-element.13), kind=kLoop, calls=%fused_computation.15 | loop fusion | flops 12800 | bytes 76808 | tf_op jit(solution)/shard_map/mul | solution.py:28
  56.1 0.1 subtract_multiply_fusion
  56.2 4.4 %multiply_add_fusion = f32[32,100,100]{2,1,0:T(8,128)} fusion(f32[32,100]{1,0:T(8,128)S(1)} %get-tuple-element.14, f32[32,100]{1,0:T(8,128)S(1)} %get-tuple-element.15, f32[8,32,100]{2,1,0:T(8,128)S(1)} %subtract_multiply_fusion), kind=kOutput, calls=%fused_computation.1 | convolution fusion | flops 31360000 | bytes 1408000 | tf_op jit(solution)/shard_map/gpc,gpd->pcd/dot_general | solution.py:20
  60.6 0.0 all-reduce.3.cloned.1.call-update
  61.3 58.5 %all-reduce.3.cloned.1.call-done = f32[32,100,100]{2,1,0:T(8,128)} async-done(((f32[32,100,100]{2,1,0:T(8,128)}), f32[32,100,100]{2,1,0:T(8,128)}) %all-reduce.3.cloned.1.call-update) | async-done | bytes 1280016 | tf_op jit(solution)/shard_map/psum | solution.py:57
  119.8 1.6 %divide_add_fusion = f32[32,100,100]{2,1,0:T(8,128)S(1)} fusion(f32[32,100,100]{2,1,0:T(8,128)} %all-reduce.3.cloned.1.call-done, f32[100,100]{1,0:T(8,128)S(1)} %fusion.5, f32[]{:T(128)S(6)} %sub.17), kind=kLoop, calls=%fused_computation | loop fusion | flops 640000 | bytes 2600004 | tf_op jit(solution)/shard_map/add | solution.py:58
  121.4 1.5 %copy.23 = f32[32,100,100]{2,0,1:T(8,128)} copy(f32[32,100,100]{2,1,0:T(8,128)S(1)} %divide_add_fusion) | data formatting | bytes 2560000
  (3 shorter events, 0.1 us)
Async XLA Ops:
  7.2 7.1 %copy-start = (bf16[2,128,224]{1,2,0:T(8,128)(2,1)S(1)}, bf16[2,128,224]{1,2,0:T(8,128)(2,1)}, u32[]{:S(2)}) copy-start(bf16[2,128,224]{1,2,0:T(8,128)(2,1)} %param.3) | copy-start | bytes 344068
  8.4 9.7 %all-to-all-start.1 = ((bf16[1,4,1]{2,0,1:T(2,128)(2,1)}), bf16[1,4,1]{2,0,1:T(2,128)(2,1)S(1)}, u32[]{:S(2)}, u32[]{:S(2)}) async-start(bf16[1,4,1]{2,0,1:T(2,128)(2,1)} %broadcast_in_dim.2), calls=%async_computation.1 | async-start | bytes 4096 | tf_op jit(solution)/shard_map/all_to_all | solution.py:49
  18.2 8.1 %all-to-all-start = ((bf16[2,4,3200]{2,0,1:T(2,128)(2,1)}), bf16[2,4,3200]{2,0,1:T(2,128)(2,1)S(1)}, u32[]{:S(2)}, u32[]{:S(2)}) async-start(bf16[2,4,3200]{2,0,1:T(2,128)(2,1)} %copy.20), calls=%async_computation | async-start | bytes 102400 | tf_op jit(solution)/shard_map/all_to_all | solution.py:48
  21.5 98.3 %all-reduce.3.cloned.1.call-start = ((), (), s32[]{:S(2)}) async-start(), calls=%async_computation.2 | async-start | bytes 3407872 | tf_op jit(solution)/shard_map/psum | solution.py:57
Sparse Core Ops, SparseCore 0:
  60.7 59.0 all-reduce.2
where the time goes:
time: 130 us
  waiting for transfers between devices  65 us (50%)
  blocking collectives  27.4 us (21%)
  between operations  15.4 us (12%)
  starting transfers between devices  8.48 us (7%)
  other arithmetic  4.59 us (4%)
  matrix products  4.57 us (4%)
  local copies, waits for them, and re-layouts  4.13 us (3%)
    psum x1, waiting for transfers between devices, on_device(): summed = lax.psum(own_term, 'dp')  58.5 us
    psum x1, blocking collectives, common_mean(): total_count, total_sums = lax.psum((group_count, group_sums), 'dp')  27.4 us
    all_to_all x1, starting transfers between devices, on_device(): lax.all_to_all(owned_wire, 'pos', split_axis=1, concat_axis=0, tiled=True)  5.16 us
    dot_general x1, matrix products, local_stats(): jnp.einsum('gpc,gpd->pcd', centered, centered, precision=lax.Precision.HI...  4.36 us
    all_to_all x1, waiting for transfers between devices, on_device(): lax.all_to_all(packed, 'pos', split_axis=1, concat_axis=0, tiled=True)  3.88 us
    all_to_all x1, starting transfers between devices, on_device(): lax.all_to_all(packed, 'pos', split_axis=1, concat_axis=0, tiled=True)  3.28 us
    all_to_all x1, waiting for transfers between devices, on_device(): lax.all_to_all(owned_wire, 'pos', split_axis=1, concat_axis=0, tiled=True)  2.61 us
  transfers between devices with their start and end apart: 3, of which 3 were waited for; matrix products, arithmetic and copies ran while one was open for 2% of the time, Pallas kernels for 0%

commit v1 on v0

--- a/solution.py
+++ b/solution.py
@@ -1,9 +1,41 @@
+import functools
 import jax
 import jax.numpy as jnp
 from jax import lax
 from jax.sharding import PartitionSpec as P
 
 CH = 100
+
+
+def hold_frame(block_in, d_out, x0):
+    far_arr, local_now = (block_in.shape[:d_out], block_in.shape[d_out + 1 :])
+    heard = jnp.moveaxis(block_in.reshape(*far_arr, x0, -1, *local_now), d_out, 0)
+    return heard
+
+
+def make_chunk(local_values, ndim_at):
+    part_next = list(local_values.shape[1:])
+    part_next[ndim_at] *= local_values.shape[0]
+    y1 = jnp.moveaxis(local_values, 0, ndim_at).reshape(part_next)
+    return y1
+
+
+def ticks_spread(block_here, chip_axis, body, local):
+    arr_next, mixed_arr = (jax.lax.axis_size(chip_axis), jax.lax.axis_index(chip_axis))
+    z1 = hold_frame(block_here, body, arr_next)
+    m_next = z1
+    for jj in [*range(1, arr_next)]:
+        part_now, t1 = ((mixed_arr + jj) % arr_next, (mixed_arr - jj) % arr_next)
+        finding = lax.dynamic_index_in_dim(z1, part_now, 0)
+        now = jax.lax.ppermute(
+            finding, chip_axis, tuple(((idx, (idx + jj) % arr_next) for idx in range(arr_next)))
+        )
+        m_next = lax.dynamic_update_slice_in_dim(m_next, now, t1, axis=0)
+    block_next = make_chunk(m_next, local)
+    return block_next
+
+
+_bring_case = functools.partial(ticks_spread, chip_axis="pos", body=1, local=0)
 
 
 def local_stats(received, source_counts, slots, rows, width):
@@ -46,7 +78,7 @@
     owned_wire = jnp.broadcast_to(owned.astype(jnp.bfloat16).reshape(1, 1, 1), (1, groups, 1))
     received, source_counts = (
         lax.all_to_all(packed, "pos", split_axis=1, concat_axis=0, tiled=True),
-        lax.all_to_all(owned_wire, "pos", split_axis=1, concat_axis=0, tiled=True),
+        _bring_case(owned_wire),
     )
     source_counts = source_counts.reshape(groups).astype(jnp.float32)
     group_count, group_sums, group_mean, products = local_stats(

time: 130 us -> 132 us (1.015)
  starting transfers between devices: 8.48 us -> 13.2 us
  waiting for transfers between devices: 65 us -> 60.6 us
  local copies, waits for them, and re-layouts: 4.13 us -> 5.72 us
    ppermute x0 -> x3, starting transfers between devices: none -> 9.83 us  [ticks_spread(): jax.lax.ppermute(finding, chip_axis, tuple(((idx, (idx + jj) % arr_next)...]
    all_to_all x1 -> x0, starting transfers between devices: 5.16 us -> none  [on_device(): lax.all_to_all(owned_wire, 'pos', split_axis=1, concat_axis=0, tiled=True)]
    all_to_all x1 -> x0, waiting for transfers between devices: 2.61 us -> none  [on_device(): lax.all_to_all(owned_wire, 'pos', split_axis=1, concat_axis=0, tiled=True)]
    all_to_all x1, waiting for transfers between devices: 3.88 us -> 1.62 us  [on_device(): lax.all_to_all(packed, 'pos', split_axis=1, concat_axis=0, tiled=True)]
    dynamic_update_slice x0 -> x3, local copies, waits for them, and re-layouts: none -> 2.17 us  [ticks_spread(): m_next = lax.dynamic_update_slice_in_dim(m_next, now, t1, axis=0)]
  transfers between devices with their start and end apart: 3 -> 5, of which waited for: 3 -> 2; matrix products, arithmetic and copies ran while one was open for 2% -> 4% of each run, Pallas kernels for 0% -> 0%
where the time goes in v1:
time: 132 us; the launch traced here: 131 us
  waiting for transfers between devices  60.6 us (46%)
  blocking collectives  27.2 us (21%)
  between operations  15.5 us (12%)
  starting transfers between devices  13.2 us (10%)
  local copies, waits for them, and re-layouts  5.72 us (4%)
  other arithmetic  4.6 us (3%)
  matrix products  4.57 us (3%)
    psum x1, waiting for transfers between devices, on_device(): summed = lax.psum(own_term, 'dp')  58.9 us
    psum x1, blocking collectives, common_mean(): total_count, total_sums = lax.psum((group_count, group_sums), 'dp')  27.2 us
    ppermute x3, starting transfers between devices, ticks_spread(): jax.lax.ppermute(finding, chip_axis, tuple(((idx, (idx + jj) % arr_next)...  9.83 us
    dot_general x1, matrix products, local_stats(): jnp.einsum('gpc,gpd->pcd', centered, centered, precision=lax.Precision.HI...  4.37 us
    all_to_all x1, starting transfers between devices, on_device(): lax.all_to_all(packed, 'pos', split_axis=1, concat_axis=0, tiled=True)  3.28 us
  transfers between devices with their start and end apart: 5, of which 2 were waited for; matrix products, arithmetic and copies ran while one was open for 4% of the time, Pallas kernels for 0%

profile of v1, /device:TPU:0, one launch (start us, length us, event | category | flops | bytes accessed | tf_op | source)
XLA Modules:
  0.0 131.3 jit_solution(15129336794907413112)
XLA Ops:
  7.2 0.0 copy-start
  7.9 4.3 %collective-permute-start = (bf16[1,1,1,1]{3,2,1,0:T(2,128)(2,1)}, bf16[1,1,1,1]{3,2,1,0:T(2,128)(2,1)}, u32[]{:S(2)}, u32[]{:S(2)}) collective-permute-start(bf16[1,1,1,1]{3,2,1,0:T(2,128)(2,1)} %bitcast.2), channel_id=1, source_target_pairs={{0,1},{1,2},{2,3},{3,0},{4,5},{5,6},{6,7},{7,4},{8,9},{9,10},{10,1... | collective-permute-start | bytes 14 | tf_op jit(solution)/shard_map/ppermute | solution.py:30
  12.2 2.8 %collective-permute-start.1 = (bf16[1,1,1,1]{3,2,1,0:T(2,128)(2,1)}, bf16[1,1,1,1]{3,2,1,0:T(2,128)(2,1)}, u32[]{:S(2)}, u32[]{:S(2)}) collective-permute-start(bf16[1,1,1,1]{3,2,1,0:T(2,128)(2,1)} %bitcast.2), channel_id=1, source_target_pairs={{0,2},{1,3},{2,0},{3,1},{4,6},{5,7},{6,4},{7,5},{8,10},{9,11},{10,... | collective-permute-start | bytes 14 | tf_op jit(solution)/shard_map/ppermute | solution.py:30
  15.0 2.7 %collective-permute-start.2 = (bf16[1,1,1,1]{3,2,1,0:T(2,128)(2,1)}, bf16[1,1,1,1]{3,2,1,0:T(2,128)(2,1)}, u32[]{:S(2)}, u32[]{:S(2)}) collective-permute-start(bf16[1,1,1,1]{3,2,1,0:T(2,128)(2,1)} %bitcast.2), channel_id=1, source_target_pairs={{0,3},{1,0},{2,1},{3,2},{4,7},{5,4},{6,5},{7,6},{8,11},{9,8},{10,9... | collective-permute-start | bytes 14 | tf_op jit(solution)/shard_map/ppermute | solution.py:30
  17.7 0.7 slice.3
  18.4 0.0 copy-done
  18.4 0.2 fusion
  18.6 0.1 copy.13
  18.7 0.2 reshape.79
  18.9 0.1 broadcast_multiply_fusion
  19.0 0.7 copy.14
  19.7 3.3 %all-to-all-start = ((bf16[2,4,3200]{2,0,1:T(2,128)(2,1)}), bf16[2,4,3200]{2,0,1:T(2,128)(2,1)S(1)}, u32[]{:S(2)}, u32[]{:S(2)}) async-start(bf16[2,4,3200]{2,0,1:T(2,128)(2,1)} %copy.14), calls=%async_computation | async-start | bytes 102400 | tf_op jit(solution)/shard_map/all_to_all | solution.py:80
  22.9 0.0 all-reduce.3.cloned.1.call-start
  23.1 0.0 collective-permute-done
  23.1 0.7 dynamic_update_slice.12
  23.8 0.7 dynamic_update_slice.13
  24.6 0.7 dynamic_update_slice.14
  25.3 0.1 fusion.6
  25.3 0.7 convert_reduce_fusion.1
  26.0 0.1 reshape.83
  26.1 1.6 %all-to-all-done = bf16[2,4,3200]{2,0,1:T(2,128)(2,1)S(1)} async-done(((bf16[2,4,3200]{2,0,1:T(2,128)(2,1)}), bf16[2,4,3200]{2,0,1:T(2,128)(2,1)S(1)}, u32[]{:S(2)}, u32[]{:S(2)}) %all-to-all-start) | async-done | bytes 51232 | tf_op jit(solution)/shard_map/all_to_all | solution.py:80
  27.7 0.1 convert_reduce_fusion
  27.8 0.1 reduce_sum.21
  27.9 0.3 reshape.82
  28.2 27.2 %all-reduce = (f32[32,100]{1,0:T(8,128)S(1)}, f32[]{:T(128)}) all-reduce(f32[32,100]{1,0:T(8,128)S(1)} %reduce_sum.21, f32[]{:T(128)} %convert_reduce_fusion.1), channel_id=1, replica_groups=mesh['dp'=8,'pos'=4] {'dp'}, use_global_device_ids=true, to_apply=%region_1.2 | all-reduce | flops 3201 | bytes 25608 | tf_op jit(solution)/shard_map/psum | solution.py:57
  55.4 1.9 %broadcast_multiply_fusion.1 = (f32[32,100]{1,0:T(8,128)S(1)}, f32[32,100]{1,0:T(8,128)S(1)}, f32[32,100]{1,0:T(8,128)S(1)}, f32[32,100]{1,0:T(8,128)}) fusion(f32[]{:T(128)} %convert_reduce_fusion.1, f32[32,100]{1,0:T(8,128)S(1)} %reduce_sum.21, f32[32,100]{1,0:T(8,128)S(1)} %get-tuple-element.8, f32[]{:T(128)} %get-tuple-element.9), kind=kLoop, calls=%fused_computation.15 | loop fusion | flops 12800 | bytes 76808 | tf_op jit(solution)/shard_map/mul | solution.py:60
  57.3 0.1 subtract_multiply_fusion
  57.4 4.4 %multiply_add_fusion = f32[32,100,100]{2,1,0:T(8,128)} fusion(f32[32,100]{1,0:T(8,128)S(1)} %get-tuple-element.10, f32[32,100]{1,0:T(8,128)S(1)} %get-tuple-element.11, f32[8,32,100]{2,1,0:T(8,128)S(1)} %subtract_multiply_fusion), kind=kOutput, calls=%fused_computation.1 | convolution fusion | flops 31360000 | bytes 1408000 | tf_op jit(solution)/shard_map/gpc,gpd->pcd/dot_general | solution.py:52
  61.8 0.0 all-reduce.3.cloned.1.call-update
  62.5 58.9 %all-reduce.3.cloned.1.call-done = f32[32,100,100]{2,1,0:T(8,128)} async-done(((f32[32,100,100]{2,1,0:T(8,128)}), f32[32,100,100]{2,1,0:T(8,128)}) %all-reduce.3.cloned.1.call-update) | async-done | bytes 1280016 | tf_op jit(solution)/shard_map/psum | solution.py:89
  121.4 1.6 %divide_add_fusion = f32[32,100,100]{2,1,0:T(8,128)S(1)} fusion(f32[32,100,100]{2,1,0:T(8,128)} %all-reduce.3.cloned.1.call-done, f32[100,100]{1,0:T(8,128)S(1)} %fusion.5, f32[]{:T(128)S(6)} %sub.29), kind=kLoop, calls=%fused_computation | loop fusion | flops 640000 | bytes 2600004 | tf_op jit(solution)/shard_map/add | solution.py:90
  123.0 1.5 %copy.17 = f32[32,100,100]{2,0,1:T(8,128)} copy(f32[32,100,100]{2,1,0:T(8,128)S(1)} %divide_add_fusion) | data formatting | bytes 2560000
  (7 shorter events, 0.1 us)
Async XLA Ops:
  7.2 11.2 %copy-start = (bf16[2,128,224]{1,2,0:T(8,128)(2,1)S(1)}, bf16[2,128,224]{1,2,0:T(8,128)(2,1)}, u32[]{:S(2)}) copy-start(bf16[2,128,224]{1,2,0:T(8,128)(2,1)} %param.3) | copy-start | bytes 344068
  7.9 15.2 %collective-permute-start = (bf16[1,1,1,1]{3,2,1,0:T(2,128)(2,1)}, bf16[1,1,1,1]{3,2,1,0:T(2,128)(2,1)}, u32[]{:S(2)}, u32[]{:S(2)}) collective-permute-start(bf16[1,1,1,1]{3,2,1,0:T(2,128)(2,1)} %bitcast.2), channel_id=1, source_target_pairs={{0,1},{1,2},{2,3},{3,0},{4,5},{5,6},{6,7},{7,4},{8,9},{9,10},{10,1... | collective-permute-start | bytes 14 | tf_op jit(solution)/shard_map/ppermute | solution.py:30
  12.2 11.7 %collective-permute-start.1 = (bf16[1,1,1,1]{3,2,1,0:T(2,128)(2,1)}, bf16[1,1,1,1]{3,2,1,0:T(2,128)(2,1)}, u32[]{:S(2)}, u32[]{:S(2)}) collective-permute-start(bf16[1,1,1,1]{3,2,1,0:T(2,128)(2,1)} %bitcast.2), channel_id=1, source_target_pairs={{0,2},{1,3},{2,0},{3,1},{4,6},{5,7},{6,4},{7,5},{8,10},{9,11},{10,... | collective-permute-start | bytes 14 | tf_op jit(solution)/shard_map/ppermute | solution.py:30
  15.0 9.6 %collective-permute-start.2 = (bf16[1,1,1,1]{3,2,1,0:T(2,128)(2,1)}, bf16[1,1,1,1]{3,2,1,0:T(2,128)(2,1)}, u32[]{:S(2)}, u32[]{:S(2)}) collective-permute-start(bf16[1,1,1,1]{3,2,1,0:T(2,128)(2,1)} %bitcast.2), channel_id=1, source_target_pairs={{0,3},{1,0},{2,1},{3,2},{4,7},{5,4},{6,5},{7,6},{8,11},{9,8},{10,9... | collective-permute-start | bytes 14 | tf_op jit(solution)/shard_map/ppermute | solution.py:30
  19.7 8.1 %all-to-all-start = ((bf16[2,4,3200]{2,0,1:T(2,128)(2,1)}), bf16[2,4,3200]{2,0,1:T(2,128)(2,1)S(1)}, u32[]{:S(2)}, u32[]{:S(2)}) async-start(bf16[2,4,3200]{2,0,1:T(2,128)(2,1)} %copy.14), calls=%async_computation | async-start | bytes 102400 | tf_op jit(solution)/shard_map/all_to_all | solution.py:80
  22.9 98.5 %all-reduce.3.cloned.1.call-start = ((), (), s32[]{:S(2)}) async-start(), calls=%async_computation.1 | async-start | bytes 3407872 | tf_op jit(solution)/shard_map/psum | solution.py:89
Sparse Core Ops, SparseCore 0:
  61.9 59.4 all-reduce.2
